TPU v7x, 32 devices: a whole 2x2x4 slice. The times are simulated.
32 devices in a mesh: req: 8 (over z, x), tp: 4 (over y, core).
Axes of the slice: x: 2, y: 2, z: 4, core: 2. Of those that a mesh axis runs over, the one named last changes fastest.
Arguments:
- layer_in: bfloat16 [4, 64, 2880], P(None, 'req'), may hold values from -3 to 3
- query_in: bfloat16 [4, 64, 2048], P(None, 'req', 'tp'), may hold values from -6 to 6
- unrotated_key: bfloat16 [4, 64, 512], P(None, 'req', 'tp'), may hold values from -6 to 6
- incoming_value: bfloat16 [4, 64, 512], P(None, 'req', 'tp'), may hold values from -12 to 12
- rotated_prompt_keys: bfloat16 [64, 256, 512], P('req', None, 'tp'), may hold values from -270 to 270
- prompt_value_rows: bfloat16 [64, 256, 512], P('req', None, 'tp'), may hold values from -6 to 6
- generated_key_rows: bfloat16 [64, 64, 512], P('req', None, 'tp'), may hold values from -9 to 9
- generated_value_rows: bfloat16 [64, 64, 512], P('req', None, 'tp'), may hold values from -12 to 12
- lengths: int32 [8], replicated, may hold values from 128 to 2048, as said below
- parents: int32 [4, 8, 8], replicated, may hold values from 0 to 7
- routes: int32 [4, 64, 4], P(None, 'req'), may hold values from 0 to 15, all different within a row; in each aligned block of 8 rows (0 to 7, 8 to 15, ..., all dimensions but the last counted through in order) at most 4 rows name the same one
- head_sink_logits: float32 [32], P('tp'), may hold values from 1 to 6
- out_weight: bfloat16 [2048, 2880], P('tp'), may hold values from -0.5 to 0.5
- mlp_gain: float32 [2880], replicated, may hold values from 0.5 to 1.5
- router_weight: bfloat16 [2880, 16], replicated, may hold values from -0.21875 to 0.21875
- expert_gate: bfloat16 [16, 2880, 2880], P('req', None, 'tp'), may hold values from -0.4375 to 0.4375
- expert_up: bfloat16 [16, 2880, 2880], P('req', None, 'tp'), may hold values from -0.4375 to 0.4375
- expert_down: bfloat16 [16, 2880, 2880], P('req', 'tp'), may hold values from -0.109375 to 0.109375
- next_gain: float32 [2880], replicated, may hold values from 0.5 to 1.5
- next_q_weight: bfloat16 [2880, 2048], P(None, 'tp'), may hold values from -0.109375 to 0.109375
- following_key_value_weight: bfloat16 [2880, 2, 512], P(None, None, 'tp'), may hold values from -0.109375 to 0.109375
Outputs:
- layer_out: bfloat16 [4, 64, 2880], P(None, 'req')
- next_query: bfloat16 [4, 64, 2048], P(None, 'req', 'tp')
- next_keyval: bfloat16 [4, 64, 2, 512], P(None, 'req', None, 'tp')
Inputs may be any that keep to these rules, and one draw needn't show every extreme that they name: `lengths`: some group's prompt holds exactly 2048 positions. `routes`: a row names 4 different experts; in the rows of one device at one step no expert is named more than 4 times, a bound that some block reaches.
All inputs are finite; a program needn't handle non-finite values.
Results may differ from a plain program's by a relative error of at most 0.029.
Values may be sent and summed in bfloat16 or wider, within the bound.
A program may use at most 128 MiB of HBM per device.

v0:
```python
import jax
import jax.numpy as jnp
from jax import lax
from jax.sharding import PartitionSpec as P

HEAD = 64
EXPERTS = 16
THETA = 150000.0
EPS = 1e-05
NEG = -1e30
BF = jnp.bfloat16
F32 = jnp.float32


def rope(vectors, positions):
    half = HEAD // 2
    powers = jnp.arange(half, dtype=F32) * (2.0 / HEAD)
    angles = positions.astype(F32)[..., None, None] * jnp.power(THETA, -powers)
    cos, sin = jnp.cos(angles), jnp.sin(angles)
    lower, upper = vectors[..., :half], vectors[..., half:]
    return jnp.concatenate([lower * cos - upper * sin, lower * sin + upper * cos], axis=-1)


def rms(rows, gain):
    return rows * lax.rsqrt(jnp.mean(rows * rows, axis=-1, keepdims=True) + EPS) * gain


def lineage_tables(parents):
    steps, groups, beams = parents.shape
    ident = jnp.broadcast_to(jnp.arange(beams, dtype=jnp.int32), (groups, beams))
    first = []
    tokens = [[None] * steps for _ in range(steps)]
    for t in range(steps):
        walker = ident
        for s in range(t, -1, -1):
            tokens[s][t] = walker
            hot = walker[..., None] == jnp.arange(beams, dtype=jnp.int32)
            walker = jnp.sum(jnp.where(hot, parents[s][:, None, :], 0), axis=-1)
        first.append(walker)
        for s in range(t + 1, steps):
            tokens[s][t] = jnp.full_like(ident, -1)
    return jnp.stack(first), jnp.stack([jnp.stack(row) for row in tokens])


def local(
    layer_in, query_in, key_in, value_in, prompt_keys, prompt_values, gen_keys, gen_values,
    lengths, parents, routes, sinks, out_weight, mlp_gain, router_weight,
    expert_gate, expert_up, expert_down, next_gain, next_q_weight, next_kv_weight,
):
    req_count = lax.axis_size("req")
    me = lax.axis_index("req")
    T, B, q_width = query_in.shape
    kv_width = key_in.shape[2]
    K = kv_width // HEAD
    R = q_width // kv_width
    J = parents.shape[2]
    span = req_count // J
    beam = me // span
    start = me % span * B
    groups = [[c + span * j for j in range(J)] for c in range(span)]
    if span == 1:
        groups = None
    lens = lax.dynamic_slice_in_dim(lengths, start, B)
    pars = lax.dynamic_slice_in_dim(parents, start, B, axis=1)
    S = prompt_keys.shape[1]
    G = gen_keys.shape[1]
    pos = lens[None, :] + G + jnp.arange(T, dtype=jnp.int32)[:, None]
    q = rope(query_in.astype(F32).reshape(T, B, K * R, HEAD), pos).astype(BF).reshape(T, B, q_width)
    k = rope(key_in.astype(F32).reshape(T, B, K, HEAD), pos).astype(BF).reshape(T, B, kv_width)
    q_all = lax.all_gather(q, "req", axis_index_groups=groups)
    first, tokens = lineage_tables(pars)
    prompt_ok = (beam * S + jnp.arange(S, dtype=jnp.int32))[None, :] < lens[:, None]
    mask = jnp.concatenate(
        [
            jnp.broadcast_to(prompt_ok[:, None, None, :], (B, J, T, S)),
            jnp.broadcast_to((first == beam).transpose(1, 2, 0)[..., None], (B, J, T, G)),
            (tokens == beam).transpose(2, 3, 1, 0),
        ],
        axis=-1,
    )
    keys = jnp.concatenate([prompt_keys, gen_keys, k.transpose(1, 0, 2)], axis=1)
    values = jnp.concatenate([prompt_values, gen_values, value_in.transpose(1, 0, 2)], axis=1)
    keys = keys.reshape(B, S + G + T, K, HEAD)
    values = values.reshape(B, S + G + T, K, HEAD)
    qs = q_all.reshape(J, T, B, K, R, HEAD)
    scores = jnp.einsum("jtbkrd,bskd->bkjtrs", qs, keys, preferred_element_type=F32) * 0.125
    usable = mask[:, None, :, :, None, :]
    scores = jnp.where(usable, scores, NEG)
    high = jnp.max(scores, axis=-1)
    weights = jnp.where(usable, jnp.exp(scores - high[..., None]), 0.0)
    total = jnp.sum(weights, axis=-1)
    part = jnp.einsum("bkjtrs,bskd->jtbkrd", weights.astype(BF), values, preferred_element_type=F32)
    high = high.transpose(2, 3, 0, 1, 4)
    total = total.transpose(2, 3, 0, 1, 4)
    part = (part / jnp.maximum(total, 1e-30)[..., None]).astype(BF)
    stats = jnp.stack([high, total], axis=1)
    part = lax.all_to_all(part, "req", 0, 0, axis_index_groups=groups)
    stats = lax.all_to_all(stats, "req", 0, 0, axis_index_groups=groups)
    high, total = stats[:, 0], stats[:, 1]
    sink = sinks.reshape(K, R)
    peak = jnp.maximum(jnp.max(high, axis=0), sink)
    share = total * jnp.exp(high - peak)
    bottom = jnp.sum(share, axis=0) + jnp.exp(sink - peak)
    attended = jnp.sum(part.astype(F32) * (share / bottom)[..., None], axis=0)
    attended = attended.astype(BF).reshape(T * B, q_width)
    projected = jnp.dot(attended, out_weight, preferred_element_type=F32)
    x1 = layer_in.reshape(T * B, -1).astype(F32) + lax.psum(projected.astype(BF), "tp").astype(F32)
    h2 = rms(x1, mlp_gain).astype(BF)
    logits = jnp.dot(h2, router_weight, preferred_element_type=F32)
    hot = jnp.sum(
        (routes.reshape(T * B, -1, 1) == jnp.arange(EXPERTS, dtype=jnp.int32)).astype(F32), axis=1
    )
    masked = jnp.where(hot > 0, logits, NEG)
    raw = jnp.where(hot > 0, jnp.exp(masked - jnp.max(masked, axis=-1, keepdims=True)), 0.0)
    gates = raw / jnp.sum(raw, axis=-1, keepdims=True)
    h2_all = lax.all_gather(h2, "req", tiled=True)
    gates_all = lax.all_gather(gates, "req", tiled=True)
    slabs = expert_gate.shape[0]
    split = slabs * req_count // EXPERTS
    moe = 0.0
    for s in range(slabs):
        expert = (me * slabs + s) // split
        weight = lax.dynamic_slice_in_dim(gates_all, expert, 1, axis=1)
        gate = jnp.minimum(jnp.dot(h2_all, expert_gate[s], preferred_element_type=F32), 7.0)
        up = jnp.clip(jnp.dot(h2_all, expert_up[s], preferred_element_type=F32), -7.0, 7.0)
        hidden = ((up + 1.0) * gate * jax.nn.sigmoid(1.702 * gate) * weight).astype(BF)
        moe = moe + jnp.dot(hidden, expert_down[s], preferred_element_type=F32)
    moe = lax.psum_scatter(moe.astype(BF), "req", scatter_dimension=0, tiled=True)
    moe = lax.psum(moe, "tp").astype(F32)
    x2 = x1 + moe
    h3 = rms(x2, next_gain).astype(BF)
    next_query = jnp.dot(h3, next_q_weight, preferred_element_type=F32).astype(BF)
    next_kv = jnp.einsum("nd,dcf->ncf", h3, next_kv_weight, preferred_element_type=F32).astype(BF)
    return (
        x2.astype(BF).reshape(T, B, -1),
        next_query.reshape(T, B, q_width),
        next_kv.reshape(T, B, 2, kv_width),
    )


def solution(mesh):
    placed = (
        P(None, "req", None), P(None, "req", "tp"), P(None, "req", "tp"), P(None, "req", "tp"),
        P("req", None, "tp"), P("req", None, "tp"), P("req", None, "tp"), P("req", None, "tp"),
        P(), P(), P(None, "req", None), P("tp"), P("tp", None), P(), P(),
        P("req", None, "tp"), P("req", None, "tp"), P("req", "tp", None),
        P(), P(None, "tp"), P(None, None, "tp"),
    )
    return jax.shard_map(
        local, mesh=mesh, in_specs=placed,
        out_specs=(P(None, "req", None), P(None, "req", "tp"), P(None, "req", None, "tp")),
        check_vma=False,
    )
```

profile of v0, /device:TPU:0, one launch (start us, length us, event | category | flops | bytes accessed | tf_op | source)
XLA Modules:
  0.0 316.0 jit_solution(11140793845565401066)
XLA Ops:
  14.3 34.5 %all_gather.9 = bf16[8,4,8,512]{3,2,1,0:T(8,128)(2,1)} all-gather(bf16[1,4,8,512]{3,2,1,0:T(8,128)(2,1)S(1)} %convert_element_type.87), channel_id=1, replica_groups=mesh['req'=8,'tp'=4] {'req'}, dimensions={0}, use_global_device_ids=true | all-gather | bytes 294912 | tf_op jit(solution)/shard_map/all_gather | solution.py:70
  48.8 1.3 reshape.181
  50.1 2.0 pad_maximum_fusion.1
  52.1 2.2 copy.122
  54.6 2.0 fusion.24
  56.7 1.6 copy-done.1
  58.3 1.3 fusion.25
  60.4 1.3 copy.125
  62.6 5.5 %all-to-all-start.1 = ((f32[8,1,512]{2,1,0:T(1,128)}), f32[8,1,512]{2,1,0:T(1,128)S(1)}, u32[]{:S(2)}, u32[]{:S(2)}) async-start(f32[8,1,512]{2,1,0:T(1,128)} %reshape.201), calls=%async_computation.1 | async-start | bytes 32768 | tf_op jit(solution)/shard_map/all_to_all | solution.py:98
  68.1 2.0 pad_maximum_fusion
  70.1 2.2 copy.115
  72.4 3.9 %divide_convert_fusion = bf16[8,4,8,2,4,64]{5,0,4,1,3,2:T(8,128)(2,1)} fusion(bf16[8,324,2,64,1,1]{1,3,5,4,2,0:T(8,128)(2,1)} %bitcast.191, f32[8,2,8,4,4,324]{5,2,4,3,1,0:T(8,128)} %copy-done.1, f32[8,2,8,4,4]{2,4,3,1,0:T(4,128)S(1)} %copy-done.6, pred[8,8,4,324]{3,1,2,0:T(8,128)(4,1)} %copy-done.7, f32[8,4,8,2,4]{0,4,1,3,2:T(4,128)S(1)} %bitcast_maximum_fusion), kind=kOutput, calls=%fused_computation.55 | convolution fusion | flops 88514560 | bytes 3679232 | tf_op jit(solution)/shard_map/bkjtrs,bskd->jtbkrd/dot_general | solution.py:92
  76.3 1.2 copy.157
  78.7 6.0 %all-to-all-start = ((bf16[8,2,8192]{2,1,0:T(2,128)(2,1)}), bf16[8,2,8192]{2,1,0:T(2,128)(2,1)}, u32[]{:S(2)}, u32[]{:S(2)}) async-start(bf16[8,2,8192]{2,1,0:T(2,128)(2,1)} %reshape.199), calls=%async_computation | async-start | bytes 524288 | tf_op jit(solution)/shard_map/all_to_all | solution.py:97
  87.1 5.9 %all-to-all-done = bf16[8,2,8192]{2,1,0:T(2,128)(2,1)} async-done(((bf16[8,2,8192]{2,1,0:T(2,128)(2,1)}), bf16[8,2,8192]{2,1,0:T(2,128)(2,1)}, u32[]{:S(2)}, u32[]{:S(2)}) %all-to-all-start) | async-done | bytes 262176 | tf_op jit(solution)/shard_map/all_to_all | solution.py:97
  93.0 2.1 reshape.200
  95.1 1.7 multiply_reduce_fusion
  97.0 1.6 convolution_convert_fusion
  98.7 29.9 %all-reduce.3.cloned.1.call-done = bf16[32,2880]{1,0:T(8,128)(2,1)} async-done(((bf16[32,2880]{1,0:T(8,128)(2,1)}), bf16[32,2880]{1,0:T(8,128)(2,1)}) %all-reduce.3.cloned.1.call-update) | async-done | bytes 184336 | tf_op jit(solution)/shard_map/psum | solution.py:107
  129.8 1.7 multiply_convert_fusion.1
  132.8 30.8 %all-gather = f32[8,32,16]{1,2,0:T(8,128)S(1)} all-gather(f32[1,32,16]{1,2,0:T(8,128)S(1)} %divide_bitcast_fusion), channel_id=1, replica_groups=mesh['req'=8,'tp'=4] {'req'}, dimensions={0}, use_global_device_ids=true | all-gather | bytes 18432 | tf_op jit(solution)/shard_map/all_gather | solution.py:117
  163.8 11.5 %all-gather.3.cloned.1.call-done = bf16[256,2880]{1,0:T(8,128)(2,1)} async-done(((bf16[32,2880]{1,0:T(8,128)(2,1)}), bf16[256,2880]{1,0:T(8,128)(2,1)}) %all-gather.3.cloned.1.call-update) | async-done | bytes 1474576 | tf_op jit(solution)/shard_map/all_gather | solution.py:116
  175.3 5.0 %fusion.48 = f32[256,720]{0,1:T(8,128)} fusion(bf16[256,2880]{1,0:T(8,128)(2,1)} %all-gather.3.cloned.1.call-done, bf16[2,2880,720]{1,2,0:T(8,128)(2,1)} %param.36), kind=kOutput, calls=%fused_computation.38 | convolution fusion | flops 1061867520 | bytes 6483968 | tf_op jit(solution)/shard_map/dot_general | solution.py:124
  180.3 4.4 %fusion.42 = f32[256,720]{0,1:T(8,128)} fusion(bf16[256,2880]{1,0:T(8,128)(2,1)S(1)} %copy-done.13, bf16[2,2880,720]{1,2,0:T(8,128)(2,1)} %param.36), kind=kOutput, calls=%fused_computation.36 | convolution fusion | flops 1061867520 | bytes 6451200 | tf_op jit(solution)/shard_map/dot_general | solution.py:124
  184.7 10.7 %fusion = f32[256,2880]{1,0:T(8,128)} fusion(bf16[2,720,2880]{2,1,0:T(8,128)(2,1)} %param.38, f32[256,720]{0,1:T(8,128)} %fusion.48, bf16[256,2880]{1,0:T(8,128)(2,1)} %all-gather.3.cloned.1.call-done, bf16[2,2880,720]{1,2,0:T(8,128)(2,1)} %param.37, f32[256]{0:T(256)S(1)} %bitcast.205), kind=kOutput, calls=%fused_computation | convolution fusion | flops 2125209600 | bytes 13673472 | tf_op jit(solution)/shard_map/dot_general | solution.py:127
  195.3 11.1 %fusion.21 = bf16[256,2880]{1,0:T(8,128)(2,1)} fusion(f32[256,2880]{1,0:T(8,128)} %fusion, bf16[2,720,2880]{2,1,0:T(8,128)(2,1)} %param.38, f32[256,720]{0,1:T(8,128)} %fusion.42, bf16[256,2880]{1,0:T(8,128)(2,1)} %all-gather.3.cloned.1.call-done, bf16[2,2880,720]{1,2,0:T(8,128)(2,1)} %param.37, f32[256]{0:T(256)S(1)} %bitcast.204), kind=kOutput, calls=%fused_computation.19 | convolution fusion | flops 2126684160 | bytes 15213568 | tf_op jit(solution)/shard_map/dot_general | solution.py:127
  206.5 63.7 %reduce-scatter.2.cloned.1.call-done = bf16[32,2880]{1,0:T(8,128)(2,1)} async-done(((bf16[256,2880]{1,0:T(8,128)(2,1)}), bf16[32,2880]{1,0:T(8,128)(2,1)}) %reduce-scatter.2.cloned.1.call-update) | async-done | bytes 184336 | tf_op jit(solution)/shard_map/reduce_scatter | solution.py:128
  270.2 32.6 %all-reduce.5.cloned.1.call-done = bf16[32,2880]{1,0:T(8,128)(2,1)} async-done(((bf16[32,2880]{1,0:T(8,128)(2,1)}), bf16[32,2880]{1,0:T(8,128)(2,1)}) %all-reduce.5.cloned.1.call-update) | async-done | bytes 184336 | tf_op jit(solution)/shard_map/psum | solution.py:129
  302.9 1.3 multiply_reduce_fusion.1
  304.2 1.7 multiply_convert_fusion
  305.9 1.7 fusion.85
  307.6 1.2 fusion.81
  (104 shorter events, 15.9 us)
Async XLA Ops:
  7.2 89.8 %copy-start = (bf16[512,2880]{0,1:T(8,128)(2,1)S(1)}, bf16[512,2880]{0,1:T(8,128)(2,1)}, u32[]{:S(2)}) copy-start(bf16[512,2880]{0,1:T(8,128)(2,1)} %param.33) | copy-start | bytes 8847364
  54.6 5.0 %copy-start.7 = (pred[8,8,4,324]{3,1,2,0:T(8,128)(4,1)}, pred[8,8,4,324]{3,1,2,0:T(8,128)(4,1)S(1)}, u32[]{:S(2)}) copy-start(pred[8,8,4,324]{3,1,2,0:T(8,128)(4,1)S(1)} %pad_add_fusion) | copy-start | bytes 248836
  56.7 1.7 copy-start.1
  56.7 2.9 copy-start.5
  56.7 11.4 %copy-start.11 = (bf16[4,8,128]{2,1,0:T(8,128)(2,1)S(1)}, bf16[4,8,128]{2,1,0:T(8,128)(2,1)}, u32[]{:S(2)}) copy-start(bf16[4,8,128]{2,1,0:T(8,128)(2,1)} %param.24) | copy-start | bytes 24580
  60.4 12.0 %copy-start.6 = (f32[8,2,8,4,4]{2,4,3,1,0:T(4,128)S(1)}, f32[8,2,8,4,4]{2,4,3,1,0:T(4,128)}, u32[]{:S(2)}) copy-start(f32[8,2,8,4,4]{2,4,3,1,0:T(4,128)} %copy-done.5) | copy-start | bytes 24580
  62.6 16.1 %all-to-all-start.1 = ((f32[8,1,512]{2,1,0:T(1,128)}), f32[8,1,512]{2,1,0:T(1,128)S(1)}, u32[]{:S(2)}, u32[]{:S(2)}) async-start(f32[8,1,512]{2,1,0:T(1,128)} %reshape.201), calls=%async_computation.1 | async-start | bytes 32768 | tf_op jit(solution)/shard_map/all_to_all | solution.py:98
  72.4 3.9 %copy-start.14 = (f32[8]{0:T(128)S(1)}, f32[8]{0:T(128)}, u32[]{:S(2)}) copy-start(f32[8]{0:T(128)} %param.32) | copy-start | bytes 100
  78.7 14.3 %all-to-all-start = ((bf16[8,2,8192]{2,1,0:T(2,128)(2,1)}), bf16[8,2,8192]{2,1,0:T(2,128)(2,1)}, u32[]{:S(2)}, u32[]{:S(2)}) async-start(bf16[8,2,8192]{2,1,0:T(2,128)(2,1)} %reshape.199), calls=%async_computation | async-start | bytes 524288 | tf_op jit(solution)/shard_map/all_to_all | solution.py:97
  84.7 44.0 %all-reduce.3.cloned.1.call-start = ((), (), s32[]{:S(2)}) async-start(), calls=%async_computation.3 | async-start | bytes 376832 | tf_op jit(solution)/shard_map/psum | solution.py:107
  86.4 42.3 %copy-start.2 = (bf16[4,8,2880]{2,1,0:T(8,128)(2,1)S(1)}, bf16[4,8,2880]{2,1,0:T(8,128)(2,1)}, u32[]{:S(2)}) copy-start(bf16[4,8,2880]{2,1,0:T(8,128)(2,1)} %param.21) | copy-start | bytes 552964
  86.6 43.2 %copy-start.10 = (f32[2880]{0:T(1024)S(1)}, f32[2880]{0:T(1024)}, u32[]{:S(2)}) copy-start(f32[2880]{0:T(1024)} %param.34) | copy-start | bytes 34564
  87.1 44.5 %copy-start.12 = (s32[4,8,4]{1,2,0:T(4,128)S(1)}, s32[4,8,4]{1,2,0:T(4,128)}, u32[]{:S(2)}) copy-start(s32[4,8,4]{1,2,0:T(4,128)} %param.31) | copy-start | bytes 1540
  87.1 44.6 %copy-start.8 = (bf16[2880,16]{0,1:T(8,128)(2,1)S(1)}, bf16[2880,16]{0,1:T(8,128)(2,1)}, u32[]{:S(2)}) copy-start(bf16[2880,16]{0,1:T(8,128)(2,1)} %param.35) | copy-start | bytes 276484
  98.6 76.6 %all-gather.3.cloned.1.call-start = ((), (), s32[]{:S(2)}) async-start(), calls=%async_computation.4 | async-start | bytes 1695744 | tf_op jit(solution)/shard_map/all_gather | solution.py:116
  131.5 138.7 %reduce-scatter.2.cloned.1.call-start = ((), (), s32[]{:S(2)}) async-start(), calls=%async_computation.5 | async-start | bytes 1695744 | tf_op jit(solution)/shard_map/reduce_scatter | solution.py:128
  175.3 5.0 %copy-start.13 = (bf16[256,2880]{1,0:T(8,128)(2,1)S(1)}, bf16[256,2880]{1,0:T(8,128)(2,1)}, u32[]{:S(2)}) copy-start(bf16[256,2880]{1,0:T(8,128)(2,1)} %all-gather.3.cloned.1.call-done) | copy-start | bytes 4423684
  195.3 107.5 %copy-start.3 = (bf16[32,2880]{1,0:T(8,128)(2,1)S(1)}, bf16[32,2880]{1,0:T(8,128)(2,1)}, u32[]{:S(2)}) copy-start(bf16[32,2880]{1,0:T(8,128)(2,1)} %all-reduce.3.cloned.1.call-done) | copy-start | bytes 552964
  195.3 108.8 %copy-start.9 = (f32[2880]{0:T(1024)S(1)}, f32[2880]{0:T(1024)}, u32[]{:S(2)}) copy-start(f32[2880]{0:T(1024)} %param.39) | copy-start | bytes 34564
  206.4 96.4 %all-reduce.5.cloned.1.call-start = ((), (), s32[]{:S(2)}) async-start(), calls=%async_computation.6 | async-start | bytes 376832 | tf_op jit(solution)/shard_map/psum | solution.py:129
  302.9 4.8 %copy-start.4 = (bf16[2880,512]{1,0:T(8,128)(2,1)S(1)}, bf16[2880,512]{1,0:T(8,128)(2,1)}, u32[]{:S(2)}) copy-start(bf16[2880,512]{1,0:T(8,128)(2,1)} %param.40) | copy-start | bytes 8847364
Sparse Core Ops, SparseCore 0:
  98.8 29.8 all-reduce.2
  131.6 43.5 all-gather.2
  206.6 63.5 reduce-scatter.1
  272.4 30.4 all-reduce.4
where the time goes:
time: 317 us; the launch traced here: 316 us
  waiting for transfers between devices  144 us (45%)
  blocking collectives  65.4 us (21%)
  matrix products  42.8 us (14%)
  local copies, waits for them, and re-layouts  19.6 us (6%)
  other arithmetic  18.8 us (6%)
  between operations  14.2 us (4%)
  starting transfers between devices  11.6 us (4%)
    reduce_scatter x1, waiting for transfers between devices, local(): lax.psum_scatter(moe.astype(BF), 'req', scatter_dimension=0, tiled=True)  63.7 us
    all_gather x1, blocking collectives, local(): q_all = lax.all_gather(q, 'req', axis_index_groups=groups)  34.5 us
    psum x1, waiting for transfers between devices, local(): moe = lax.psum(moe, 'tp').astype(F32)  32.6 us
    all_gather x1, blocking collectives, local(): gates_all = lax.all_gather(gates, 'req', tiled=True)  30.8 us
    psum x1, waiting for transfers between devices, local(): lax.psum(projected.astype(BF), 'tp').astype(F32)  29.9 us
    dot_general x2, matrix products, local(): moe = moe + jnp.dot(hidden, expert_down[s], preferred_element_type=F32)  21.7 us
    all_gather x1, waiting for transfers between devices, local(): h2_all = lax.all_gather(h2, 'req', tiled=True)  11.5 us
    dot_general x2, matrix products, local(): jnp.dot(h2_all, expert_gate[s], preferred_element_type=F32)  9.4 us
  transfers between devices with their start and end apart: 6, of which 5 were waited for; matrix products, arithmetic and copies ran while one was open for 5% of the time, Pallas kernels for 0%

commit v1 on v0

--- a/solution.py
+++ b/solution.py
@@ -1,6 +1,10 @@
+import functools
+
 import jax
 import jax.numpy as jnp
 from jax import lax
+from jax.experimental import pallas as pl
+from jax.experimental.pallas import tpu as pltpu
 from jax.sharding import PartitionSpec as P
 
 HEAD = 64
@@ -40,6 +44,276 @@
         for s in range(t + 1, steps):
             tokens[s][t] = jnp.full_like(ident, -1)
     return jnp.stack(first), jnp.stack([jnp.stack(row) for row in tokens])
+
+
+CH = 768
+EX = 128
+HOT0 = 16
+
+
+def tail_kernel(
+    nreq, slabs, width,
+    att_ref, lin_ref, hot_ref, wo_hbm, mg_ref, wr_ref, wg_hbm, wu_hbm, wd_hbm, ng_ref, wq_hbm, wk_hbm,
+    lo_ref, nq_ref, nk_ref,
+    wo, wg, wu, wd, wq, wk,
+    psrc, prcv, xs, gs, yall, part, rb1, sb2, rb2, sb3, rb3, x2a,
+    wsem, psnd, prsem, gsnd, grcv, ysnd, yrcv, csnd, crcv,
+    asnd, arcv, bsnd, brcv, dsnd, drcv, fsnd, frcv,
+):
+    me = lax.axis_index("req")
+    tp = lax.axis_index("tp")
+    core, yy = tp % 2, tp // 2
+    rows = att_ref.shape[0]
+
+    def peer(d):
+        return ((yy + d // 2) % 2) * 2 + (core + d % 2) % 2
+
+    def rcopy(src, dst, ssem, rsem, req, t):
+        return pltpu.make_async_remote_copy(
+            src_ref=src, dst_ref=dst, send_sem=ssem, recv_sem=rsem,
+            device_id=(req, t), device_id_type=pl.DeviceIdType.MESH,
+        )
+
+    loads = [pltpu.make_async_copy(wo_hbm, wo, wsem.at[0])]
+    for s in range(slabs):
+        loads.append(pltpu.make_async_copy(wg_hbm.at[s], wg.at[s], wsem.at[1 + 3 * s]))
+        loads.append(pltpu.make_async_copy(wu_hbm.at[s], wu.at[s], wsem.at[2 + 3 * s]))
+    for s in range(slabs):
+        loads.append(pltpu.make_async_copy(wd_hbm.at[s], wd.at[s], wsem.at[3 + 3 * s]))
+    loads.append(pltpu.make_async_copy(wq_hbm, wq, wsem.at[1 + 3 * slabs]))
+    loads.append(pltpu.make_async_copy(wk_hbm, wk, wsem.at[2 + 3 * slabs]))
+    for copy in loads:
+        copy.start()
+
+    barrier = pltpu.get_barrier_semaphore()
+    for i in range(1, nreq):
+        pl.semaphore_signal(
+            barrier, inc=1, device_id=((me + i) % nreq, tp), device_id_type=pl.DeviceIdType.MESH
+        )
+    for d in range(1, 4):
+        pl.semaphore_signal(
+            barrier, inc=1, device_id=(me, peer(d)), device_id_type=pl.DeviceIdType.MESH
+        )
+
+    spans = []
+    at = 0
+    while at < width:
+        spans.append((at, min(CH, width - at)))
+        at += CH
+
+    def blk(r):
+        return pl.ds(pl.multiple_of(r * rows, rows), rows)
+
+    loads[0].wait()
+    att = att_ref[...]
+    for c, (a, w) in enumerate(spans):
+        if w < CH:
+            psrc[c] = jnp.zeros((rows, CH), BF)
+            xs[c] = jnp.zeros((rows, CH), F32)
+            gs[c] = jnp.zeros((8, CH), F32)
+        psrc[c, :, :w] = jnp.dot(att, wo[:, a:a + w], preferred_element_type=F32).astype(BF)
+        xs[c, :, :w] = lin_ref[:, a:a + w].astype(F32)
+        gs[c, :, :w] = jnp.broadcast_to(mg_ref[:, a:a + w], (8, w))
+    pl.semaphore_wait(barrier, nreq - 1 + 3)
+    sends = []
+    for d in (2, 3, 1):
+        cp = rcopy(psrc.at[peer(d)], prcv.at[d - 1], psnd.at[d - 1], prsem.at[d - 1], me, peer(d))
+        cp.start()
+        sends.append(cp)
+    x1 = xs[tp] + psrc[tp].astype(F32)
+    for cp in sends:
+        cp.wait()
+    for d in range(3):
+        x1 = x1 + prcv[d].astype(F32)
+    xs[tp] = x1
+    lane = lax.broadcasted_iota(jnp.int32, (rows, EX), 1)
+    ssq = jnp.sum(x1 * x1, axis=1, keepdims=True)
+    high = ssq.astype(BF).astype(F32)
+    low = ssq - high
+    extra = jnp.where(lane == 0, high, jnp.where(lane == 1, low, hot_ref[...]))
+    yall[tp, blk(me), :CH] = (x1 * gs[tp][:1]).astype(BF)
+    yall[tp, blk(me), CH:] = extra.astype(BF)
+
+    sends = []
+    for i in range(1, nreq):
+        piece = yall.at[tp, blk(me)]
+        cp = rcopy(piece, piece, gsnd.at[i], grcv.at[i], (me + i) % nreq, tp)
+        cp.start()
+        sends.append(cp)
+    ty, tc, td = peer(2), peer(1), peer(3)
+    for i in range(nreq):
+        src = (me + nreq - i) % nreq
+        piece = yall.at[tp, blk(src)]
+        if i > 0:
+            rcopy(piece, piece, gsnd.at[i], grcv.at[i], (me + i) % nreq, tp).wait_recv()
+        cp = rcopy(piece, piece, ysnd.at[i], yrcv.at[i], me, ty)
+        cp.start()
+        sends.append(cp)
+        cp = rcopy(piece, piece, csnd.at[0, i], crcv.at[0, i], me, tc)
+        cp.start()
+        sends.append(cp)
+    for i in range(nreq):
+        piece = yall.at[ty, blk((me + nreq - i) % nreq)]
+        rcopy(piece, piece, ysnd.at[i], yrcv.at[i], me, ty).wait_recv()
+        cp = rcopy(piece, piece, csnd.at[1, i], crcv.at[1, i], me, tc)
+        cp.start()
+        sends.append(cp)
+    for i in range(nreq):
+        piece = yall.at[tc, blk((me + nreq - i) % nreq)]
+        rcopy(piece, piece, csnd.at[0, i], crcv.at[0, i], me, tc).wait_recv()
+        piece = yall.at[td, blk((me + nreq - i) % nreq)]
+        rcopy(piece, piece, csnd.at[1, i], crcv.at[1, i], me, tc).wait_recv()
+    for cp in sends:
+        cp.wait_send()
+
+    total = nreq * rows
+    lanes = lax.broadcasted_iota(jnp.int32, (total, EX), 1)
+    ssq = jnp.zeros((total, 1), F32)
+    logits = jnp.zeros((total, EX), F32)
+    for c, (a, w) in enumerate(spans):
+        ssq = ssq + jnp.sum(
+            jnp.where(lanes < 2, yall[c, :, CH:].astype(F32), 0.0), axis=1, keepdims=True
+        )
+        logits = logits + jnp.dot(yall[c, :, :w], wr_ref[a:a + w, :], preferred_element_type=F32)
+    scale = lax.rsqrt(ssq / width + EPS)
+    logits = logits * scale
+    hot = (lanes >= HOT0) & (yall[0, :, CH:].astype(F32) > 0.5)
+    masked = jnp.where(hot, logits, NEG)
+    raw = jnp.where(hot, jnp.exp(masked - jnp.max(masked, axis=1, keepdims=True)), 0.0)
+    gates = raw / jnp.sum(raw, axis=1, keepdims=True)
+
+    hidden = []
+    for s in range(slabs):
+        weight = jnp.sum(
+            jnp.where(lanes == HOT0 + me * slabs + s, gates, 0.0), axis=1, keepdims=True
+        )
+        loads[1 + 2 * s].wait()
+        loads[2 + 2 * s].wait()
+        gate = 0.0
+        up = 0.0
+        for c, (a, w) in enumerate(spans):
+            y = yall[c, :, :w]
+            gate = gate + jnp.dot(y, wg[s, a:a + w, :], preferred_element_type=F32)
+            up = up + jnp.dot(y, wu[s, a:a + w, :], preferred_element_type=F32)
+        gate = jnp.minimum(gate * scale, 7.0)
+        up = jnp.clip(up * scale, -7.0, 7.0)
+        sig = 1.0 / (1.0 + jnp.exp(-1.702 * gate))
+        hidden.append(((up + 1.0) * gate * sig * weight).astype(BF))
+    for s in range(slabs):
+        loads[1 + 2 * slabs + s].wait()
+    for c, (a, w) in enumerate(spans):
+        acc = 0.0
+        for s in range(slabs):
+            acc = acc + jnp.dot(hidden[s], wd[s, :, a:a + w], preferred_element_type=F32)
+        if w < CH:
+            part[c, :, w:] = jnp.zeros((total, CH - w), BF)
+        part[c, :, :w] = acc.astype(BF)
+
+    sends = []
+    for k, c in ((1, td), (0, tc)):
+        cp = rcopy(part.at[c], rb1.at[k], asnd.at[k], arcv.at[k], me, tc)
+        cp.start()
+        sends.append(cp)
+    order = list(range(1, nreq)) + [0]
+    sends[0].wait_recv()
+    for i in order:
+        b = (me + i) % nreq
+        sb2[i] = (part[ty, blk(b), :].astype(F32) + rb1[1, blk(b), :].astype(F32)).astype(BF)
+        cp = rcopy(sb2.at[i], rb2.at[i], bsnd.at[i], brcv.at[i], me, ty)
+        cp.start()
+        sends.append(cp)
+    sends[1].wait_recv()
+    moe = 0.0
+    late = []
+    for i in order:
+        b = (me + i) % nreq
+        mine = part[tp, blk(b), :].astype(F32) + rb1[0, blk(b), :].astype(F32)
+        rcopy(sb2.at[i], rb2.at[i], bsnd.at[i], brcv.at[i], me, ty).wait_recv()
+        mine = mine + rb2[i].astype(F32)
+        if i == 0:
+            moe = mine
+        else:
+            sb3[i] = mine.astype(BF)
+            cp = rcopy(sb3.at[i], rb3.at[i], dsnd.at[i], drcv.at[i], b, tp)
+            cp.start()
+            sends.append(cp)
+            late.append(cp)
+    for n, cp in enumerate(late):
+        cp.wait_recv()
+        moe = moe + rb3[n + 1].astype(F32)
+    x2a[tp] = xs[tp] + moe
+    late = []
+    for d in (2, 3, 1):
+        cp = rcopy(x2a.at[tp], x2a.at[tp], fsnd.at[d - 1], frcv.at[d - 1], me, peer(d))
+        cp.start()
+        sends.append(cp)
+    for d in range(1, 4):
+        piece = x2a.at[peer(d)]
+        rcopy(piece, piece, fsnd.at[d - 1], frcv.at[d - 1], me, peer(d)).wait_recv()
+    for cp in sends:
+        cp.wait_send()
+    ssq = jnp.zeros((rows, 1), F32)
+    for c, (a, w) in enumerate(spans):
+        x2 = x2a[c, :, :w]
+        lo_ref[:, a:a + w] = x2.astype(BF)
+        ssq = ssq + jnp.sum(x2 * x2, axis=1, keepdims=True)
+    scale = lax.rsqrt(ssq / width + EPS)
+    loads[1 + 3 * slabs].wait()
+    loads[2 + 3 * slabs].wait()
+    nq = 0.0
+    nk = 0.0
+    for c, (a, w) in enumerate(spans):
+        h3 = (x2a[c, :, :w] * scale * ng_ref[:, a:a + w]).astype(BF)
+        nq = nq + jnp.dot(h3, wq[a:a + w, :], preferred_element_type=F32)
+        nk = nk + jnp.dot(h3, wk[a:a + w, :], preferred_element_type=F32)
+    nq_ref[...] = nq.astype(BF)
+    nk_ref[...] = nk.astype(BF)
+
+
+def tail(att, lin, hot, wo, mg, wr, wg, wu, wd, ng, wq, wk, nreq):
+    rows, width = lin.shape
+    slabs, _, ff = wg.shape
+    total = nreq * rows
+    chunks = -(-width // CH)
+    vm = pl.BlockSpec(memory_space=pltpu.VMEM)
+    hb = pl.BlockSpec(memory_space=pl.ANY)
+    dma = pltpu.SemaphoreType.DMA
+    return pl.pallas_call(
+        functools.partial(tail_kernel, nreq, slabs, width),
+        out_shape=(
+            jax.ShapeDtypeStruct((rows, width), BF),
+            jax.ShapeDtypeStruct((rows, wq.shape[1]), BF),
+            jax.ShapeDtypeStruct((rows, wk.shape[1]), BF),
+        ),
+        in_specs=[vm, vm, vm, hb, vm, vm, hb, hb, hb, vm, hb, hb],
+        out_specs=(vm, vm, vm),
+        scratch_shapes=[
+            pltpu.VMEM(wo.shape, BF), pltpu.VMEM(wg.shape, BF), pltpu.VMEM(wu.shape, BF),
+            pltpu.VMEM(wd.shape, BF), pltpu.VMEM(wq.shape, BF), pltpu.VMEM(wk.shape, BF),
+            pltpu.VMEM((chunks, rows, CH), BF),
+            pltpu.VMEM((3, rows, CH), BF),
+            pltpu.VMEM((chunks, rows, CH), F32),
+            pltpu.VMEM((chunks, 8, CH), F32),
+            pltpu.VMEM((chunks, total, CH + EX), BF),
+            pltpu.VMEM((chunks, total, CH), BF),
+            pltpu.VMEM((2, total, CH), BF),
+            pltpu.VMEM((nreq, rows, CH), BF),
+            pltpu.VMEM((nreq, rows, CH), BF),
+            pltpu.VMEM((nreq, rows, CH), BF),
+            pltpu.VMEM((nreq, rows, CH), BF),
+            pltpu.VMEM((chunks, rows, CH), F32),
+            dma((3 + 3 * slabs,)), dma((3,)), dma((3,)), dma((nreq,)), dma((nreq,)),
+            dma((nreq,)), dma((nreq,)), dma((2, nreq)), dma((2, nreq)),
+            dma((2,)), dma((2,)), dma((nreq,)), dma((nreq,)), dma((nreq,)), dma((nreq,)),
+            dma((3,)), dma((3,)),
+        ],
+        compiler_params=pltpu.CompilerParams(
+            collective_id=0, has_side_effects=True, vmem_limit_bytes=58 * 2**20
+        ),
+        cost_estimate=pl.CostEstimate(
+            flops=2 * total * slabs * width * ff * 3, bytes_accessed=33 * 2**20, transcendentals=0
+        ),
+    )(att, lin, hot, wo, mg, wr, wg, wu, wd, ng, wq, wk)
 
 
 def local(
@@ -103,6 +377,19 @@
     bottom = jnp.sum(share, axis=0) + jnp.exp(sink - peak)
     attended = jnp.sum(part.astype(F32) * (share / bottom)[..., None], axis=0)
     attended = attended.astype(BF).reshape(T * B, q_width)
+    if lax.axis_size("tp") == 4 and span == 1 and expert_gate.shape[0] * req_count == EXPERTS:
+        hot = jnp.sum(
+            (routes.reshape(T * B, -1, 1) == jnp.arange(EX, dtype=jnp.int32) - HOT0).astype(F32), axis=1
+        )
+        routing = jnp.pad(router_weight, ((0, 0), (HOT0, EX - HOT0 - EXPERTS)))
+        out, nq, nk = tail(
+            attended, layer_in.reshape(T * B, -1), hot, out_weight, mlp_gain[None], routing,
+            expert_gate, expert_up, expert_down, next_gain[None], next_q_weight,
+            next_kv_weight.reshape(-1, 2 * kv_width), req_count,
+        )
+        return (
+            out.reshape(T, B, -1), nq.reshape(T, B, q_width), nk.reshape(T, B, 2, kv_width)
+        )
     projected = jnp.dot(attended, out_weight, preferred_element_type=F32)
     x1 = layer_in.reshape(T * B, -1).astype(F32) + lax.psum(projected.astype(BF), "tp").astype(F32)
     h2 = rms(x1, mlp_gain).astype(BF)

time: 317 us -> 177 us (0.56)
  waiting for transfers between devices: 144 us -> 5.88 us
  Pallas kernels: 0 us -> 54.7 us
  matrix products: 42.8 us -> 5.34 us
  blocking collectives: 65.4 us -> 32.5 us
  local copies, waits for them, and re-layouts: 19.6 us -> 52.3 us
  between operations: 14.2 us -> 0.94 us
  other arithmetic: 18.8 us -> 12 us
    reduce_scatter x1 -> x0, waiting for transfers between devices: 63.7 us -> none  [local(): lax.psum_scatter(moe.astype(BF), 'req', scatter_dimension=0, tiled=True)]
    psum x2 -> x0, waiting for transfers between devices: 62.6 us -> none  [the longest x1 32.6 us: local(): moe = lax.psum(moe, 'tp').astype(F32)]
    pallas_call x0 -> x1, Pallas kernels: none -> 54.7 us  [tail(): pl.pallas_call(functools.partial(tail_kernel, nreq, slabs, width), out_sh...]
    dot_general x8 -> x0, matrix products: 36.8 us -> none  [the longest x2 21.7 us: local(): moe = moe + jnp.dot(hidden, expert_down[s], preferred_element_type=F32)]
    unnamed x38 -> x34, local copies, waits for them, and re-layouts: 6.82 us -> 38.3 us
    all_gather x1 -> x0, blocking collectives: 30.8 us -> none  [local(): gates_all = lax.all_gather(gates, 'req', tiled=True)]
    all_gather x1 -> x0, waiting for transfers between devices: 11.5 us -> none  [local(): h2_all = lax.all_gather(h2, 'req', tiled=True)]
    convert_element_type x2 -> x0, other arithmetic: 3.41 us -> none  [the longest x1 1.71 us: local(): h3 = rms(x2, next_gain).astype(BF)]
  transfers between devices with their start and end apart: 6 -> 2, of which waited for: 5 -> 1; matrix products, arithmetic and copies ran while one was open for 5% -> 26% of each run, Pallas kernels for 0% -> 0%
where the time goes in v1:
time: 177 us; the launch traced here: 175 us
  Pallas kernels  54.7 us (31%)
  local copies, waits for them, and re-layouts  52.3 us (30%)
  blocking collectives  32.5 us (18%)
  other arithmetic  12 us (7%)
  starting transfers between devices  11.5 us (6%)
  waiting for transfers between devices  5.88 us (3%)
  matrix products  5.34 us (3%)
    pallas_call x1, Pallas kernels, tail(): pl.pallas_call(functools.partial(tail_kernel, nreq, slabs, width), out_sh...  54.7 us
    unnamed x34, local copies, waits for them, and re-layouts  38.3 us
    all_gather x1, blocking collectives, local(): q_all = lax.all_gather(q, 'req', axis_index_groups=groups)  32.5 us
    all_to_all x1, starting transfers between devices, local(): part = lax.all_to_all(part, 'req', 0, 0, axis_index_groups=groups)  6 us
    all_to_all x1, waiting for transfers between devices, local(): part = lax.all_to_all(part, 'req', 0, 0, axis_index_groups=groups)  5.88 us
    all_to_all x1, starting transfers between devices, local(): stats = lax.all_to_all(stats, 'req', 0, 0, axis_index_groups=groups)  5.52 us
  transfers between devices with their start and end apart: 2, of which 1 were waited for; matrix products, arithmetic and copies ran while one was open for 26% of the time, Pallas kernels for 0%

profile of v1, /device:TPU:0, one launch (start us, length us, event | category | flops | bytes accessed | tf_op | source)
XLA Modules:
  0.0 175.2 jit_solution(12749056278051638586)
XLA Ops:
  1.4 0.7 broadcast_compare_fusion
  2.1 0.7 slice_bitcast_fusion.4
  5.3 0.8 reshape.180
  6.4 0.9 reshape.178
  7.6 32.5 %all_gather.3 = bf16[8,4,8,512]{3,2,1,0:T(8,128)(2,1)S(1)} all-gather(bf16[1,4,8,512]{3,2,1,0:T(8,128)(2,1)S(1)} %convert_element_type.48), channel_id=1, replica_groups=mesh['req'=8,'tp'=4] {'req'}, dimensions={0}, use_global_device_ids=true | all-gather | bytes 294912 | tf_op jit(solution)/shard_map/all_gather | solution.py:344
  40.1 1.1 reshape.168
  41.2 1.0 pad_maximum_fusion.1
  42.2 1.2 copy.111
  43.6 2.2 %fusion = (f32[8,2,8,4,4]{2,4,3,1,0:T(4,128)S(1)}, f32[8,2,8,4,4,324]{5,2,4,3,1,0:T(8,128)S(1)}) fusion(pred[8,8,4,324]{3,1,2,0:T(8,128)(4,1)S(1)} %pad_add_fusion, bf16[8,324,2,64,1,1]{1,3,5,4,2,0:T(8,128)(2,1)} %bitcast.105, bf16[8,4,8,2,4,64]{5,4,3,2,1,0:T(4,128)(2,1)} %reshape.168), kind=kOutput, calls=%fused_computation.2 | convolution fusion | flops 86923264 | bytes 3671040 | tf_op jit(solution)/shard_map/jtbkrd,bskd->bkjtrs/dot_general | solution.py:360
  45.8 1.2 fusion.1
  47.0 0.8 pad_maximum_fusion.2
  47.8 1.9 %copy.114 = f32[8,2,4,8,2,4]{3,5,4,2,1,0:T(4,128)} copy(f32[8,2,4,8,2,4]{0,5,2,4,3,1:T(4,128)} %pad_maximum_fusion.2) | data formatting | bytes 32768 | tf_op jit(solution)/shard_map/stack | solution.py:370
  49.7 1.8 %reshape.186 = f32[8,1,512]{2,1,0:T(1,128)} reshape(f32[8,2,4,2,4,8]{5,4,3,2,1,0:T(4,128)} %bitcast.110) | data formatting | bytes 32768
  51.5 5.5 %all-to-all-start.1 = ((f32[8,1,512]{2,1,0:T(1,128)}), f32[8,1,512]{2,1,0:T(1,128)S(1)}, u32[]{:S(2)}, u32[]{:S(2)}) async-start(f32[8,1,512]{2,1,0:T(1,128)} %reshape.186), calls=%async_computation.1 | async-start | bytes 32768 | tf_op jit(solution)/shard_map/all_to_all | solution.py:372
  57.8 2.0 %pad_maximum_fusion = bf16[8,324,128]{2,1,0:T(8,128)(2,1)} fusion(bf16[8,4,128]{2,1,0:T(4,128)(2,1)S(1)} %bitcast.121, bf16[8,64,128]{2,1,0:T(8,128)(2,1)} %param.28, bf16[8,256,128]{2,1,0:T(8,128)(2,1)} %param.26), kind=kLoop, calls=%fused_computation.15 | loop fusion | flops 1990656 | bytes 1327104 | tf_op jit(solution)/shard_map/concatenate | solution.py:356
  59.8 2.2 %copy.104 = bf16[8,324,128]{1,2,0:T(8,128)(2,1)} copy(bf16[8,324,128]{2,1,0:T(8,128)(2,1)} %pad_maximum_fusion) | data formatting | bytes 1327104 | tf_op jit(solution)/shard_map/concatenate | solution.py:356
  62.1 3.2 %divide_convert_fusion = bf16[8,4,8,2,4,64]{5,0,4,1,3,2:T(8,128)(2,1)} fusion(bf16[8,324,2,64,1,1]{1,3,5,4,2,0:T(8,128)(2,1)} %bitcast.111, f32[8,2,8,4,4,324]{5,2,4,3,1,0:T(8,128)S(1)} %get-tuple-element.49, f32[8,2,8,4,4]{2,4,3,1,0:T(4,128)S(1)} %get-tuple-element.48, pred[8,8,4,324]{3,1,2,0:T(8,128)(4,1)S(1)} %pad_add_fusion, ...), kind=kOutput, calls=%fused_computation.14 | convolution fusion | flops 88514560 | bytes 3679232 | tf_op jit(solution)/shard_map/bkjtrs,bskd->jtbkrd/dot_general | solution.py:366
  67.2 1.2 copy.120
  68.4 2.7 %copy.143 = bf16[360,8,2,128]{3,1,2,0:T(8,128)(2,1)} copy(bf16[360,8,2,128]{3,2,1,0:T(2,128)(2,1)} %bitcast.107) | data formatting | bytes 2949120
  71.4 1.1 reshape.184
  72.4 3.0 %copy.121.wo_hbm = bf16[512,2880]{1,0:T(8,128)(2,1)} copy(bf16[512,2880]{0,1:T(8,128)(2,1)S(1)} %copy-done) | data formatting | bytes 5898240 | tf_op args[12]
  75.4 11.8 %copy.122.wg_hbm = bf16[2,2880,720]{2,1,0:T(8,128)(2,1)} copy(bf16[2,2880,720]{1,2,0:T(8,128)(2,1)} %param.36) | data formatting | bytes 16588800 | tf_op args[15]
  87.2 11.7 %copy.123.wu_hbm = bf16[2,2880,720]{2,1,0:T(8,128)(2,1)} copy(bf16[2,2880,720]{1,2,0:T(8,128)(2,1)} %param.37) | data formatting | bytes 16588800 | tf_op args[16]
  98.9 1.2 pad.4.wr_ref
  100.1 6.0 %all-to-all-start = ((bf16[8,2,8192]{2,1,0:T(2,128)(2,1)}), bf16[8,2,8192]{2,1,0:T(2,128)(2,1)S(1)}, u32[]{:S(2)}, u32[]{:S(2)}) async-start(bf16[8,2,8192]{2,1,0:T(2,128)(2,1)} %reshape.184), calls=%async_computation | async-start | bytes 524288 | tf_op jit(solution)/shard_map/all_to_all | solution.py:371
  108.5 5.9 %all-to-all-done = bf16[8,2,8192]{2,1,0:T(2,128)(2,1)S(1)} async-done(((bf16[8,2,8192]{2,1,0:T(2,128)(2,1)}), bf16[8,2,8192]{2,1,0:T(2,128)(2,1)S(1)}, u32[]{:S(2)}, u32[]{:S(2)}) %all-to-all-start) | async-done | bytes 262176 | tf_op jit(solution)/shard_map/all_to_all | solution.py:371
  114.7 0.7 multiply_reduce_fusion
  115.5 0.7 convert_element_type.54.att_ref
  116.2 54.7 %shard_map.220 = (bf16[32,2880]{1,0:T(8,128)(2,1)}, bf16[32,512]{1,0:T(8,128)(2,1)}, bf16[32,256]{1,0:T(8,128)(2,1)}) custom-call(bf16[32,512]{1,0:T(8,128)(2,1)} %convert_element_type.54.att_ref, bf16[32,2880]{1,0:T(8,128)(2,1)} %bitcast.113, f32[32,128]{1,0:T(8,128)} %convert_reduce_fusion.hot_ref, bf16[512,2880]{1,0:T(8,128)(2,1)} %copy.121.wo_hbm, ...), custom_call_target="tpu_custom_call" | custom-call | flops 6370099200 | bytes 34603008 | tf_op jit(solution)/shard_map/pallas_call | solution.py:281
  170.9 1.3 copy.124
  172.2 1.6 copy.148
  173.8 1.4 copy.149
  (74 shorter events, 9.6 us)
Async XLA Ops:
  0.6 40.6 %copy-start.3 = (bf16[8,256,128]{2,1,0:T(8,128)(2,1)S(1)}, bf16[8,256,128]{2,1,0:T(8,128)(2,1)}, u32[]{:S(2)}) copy-start(bf16[8,256,128]{2,1,0:T(8,128)(2,1)} %param.25) | copy-start | bytes 1572868
  45.8 11.9 %copy-start.7 = (bf16[4,8,128]{2,1,0:T(8,128)(2,1)S(1)}, bf16[4,8,128]{2,1,0:T(8,128)(2,1)}, u32[]{:S(2)}) copy-start(bf16[4,8,128]{2,1,0:T(8,128)(2,1)} %param.24) | copy-start | bytes 24580
  45.8 11.9 %copy-start.8 = (s32[4,8,4]{1,2,0:T(4,128)S(1)}, s32[4,8,4]{1,2,0:T(4,128)}, u32[]{:S(2)}) copy-start(s32[4,8,4]{1,2,0:T(4,128)} %param.31) | copy-start | bytes 1540
  51.5 48.6 %all-to-all-start.1 = ((f32[8,1,512]{2,1,0:T(1,128)}), f32[8,1,512]{2,1,0:T(1,128)S(1)}, u32[]{:S(2)}, u32[]{:S(2)}) async-start(f32[8,1,512]{2,1,0:T(1,128)} %reshape.186), calls=%async_computation.1 | async-start | bytes 32768 | tf_op jit(solution)/shard_map/all_to_all | solution.py:372
  62.1 3.9 %copy-start.9 = (f32[8]{0:T(128)S(1)}, f32[8]{0:T(128)}, u32[]{:S(2)}) copy-start(f32[8]{0:T(128)} %param.32) | copy-start | bytes 100
  62.1 4.0 %copy-start.5 = (f32[2880]{0:T(1024)S(1)}, f32[2880]{0:T(1024)}, u32[]{:S(2)}) copy-start(f32[2880]{0:T(1024)} %param.34) | copy-start | bytes 34564
  62.1 4.6 %copy-start.6 = (f32[2880]{0:T(1024)S(1)}, f32[2880]{0:T(1024)}, u32[]{:S(2)}) copy-start(f32[2880]{0:T(1024)} %param.39) | copy-start | bytes 34564
  62.1 5.2 %copy-start.4 = (bf16[2880,16]{0,1:T(8,128)(2,1)S(1)}, bf16[2880,16]{0,1:T(8,128)(2,1)}, u32[]{:S(2)}) copy-start(bf16[2880,16]{0,1:T(8,128)(2,1)} %param.35) | copy-start | bytes 276484
  65.2 7.2 %copy-start = (bf16[512,2880]{0,1:T(8,128)(2,1)S(1)}, bf16[512,2880]{0,1:T(8,128)(2,1)}, u32[]{:S(2)}) copy-start(bf16[512,2880]{0,1:T(8,128)(2,1)} %param.33) | copy-start | bytes 8847364
  68.4 2.7 %copy-start.2 = (bf16[8,4,8,2,4,64]{5,0,4,1,3,2:T(8,128)(2,1)S(1)}, bf16[8,4,8,2,4,64]{5,0,4,1,3,2:T(8,128)(2,1)}, u32[]{:S(2)}) copy-start(bf16[8,4,8,2,4,64]{5,0,4,1,3,2:T(8,128)(2,1)} %divide_convert_fusion) | copy-start | bytes 786436
  87.2 11.7 %copy-start.1 = (bf16[2880,16]{1,0:T(8,128)(2,1)S(1)}, bf16[2880,16]{1,0:T(8,128)(2,1)}, u32[]{:S(2)}) copy-start(bf16[2880,16]{1,0:T(8,128)(2,1)} %copy.120) | copy-start | bytes 276484
  100.1 14.2 %all-to-all-start = ((bf16[8,2,8192]{2,1,0:T(2,128)(2,1)}), bf16[8,2,8192]{2,1,0:T(2,128)(2,1)S(1)}, u32[]{:S(2)}, u32[]{:S(2)}) async-start(bf16[8,2,8192]{2,1,0:T(2,128)(2,1)} %reshape.184), calls=%async_computation | async-start | bytes 524288 | tf_op jit(solution)/shard_map/all_to_all | solution.py:371

commit v2 on v1

--- a/solution.py
+++ b/solution.py
@@ -48,7 +48,8 @@
 
 CH = 768
 EX = 128
-HOT0 = 16
+SSQ0 = 16
+NT = (((1,), (1,)), ((), ()))
 
 
 def tail_kernel(
@@ -111,7 +112,9 @@
             psrc[c] = jnp.zeros((rows, CH), BF)
             xs[c] = jnp.zeros((rows, CH), F32)
             gs[c] = jnp.zeros((8, CH), F32)
-        psrc[c, :, :w] = jnp.dot(att, wo[:, a:a + w], preferred_element_type=F32).astype(BF)
+        psrc[c, :, :w] = lax.dot_general(
+            att, wo[a:a + w, :], NT, preferred_element_type=F32
+        ).astype(BF)
         xs[c, :, :w] = lin_ref[:, a:a + w].astype(F32)
         gs[c, :, :w] = jnp.broadcast_to(mg_ref[:, a:a + w], (8, w))
     pl.semaphore_wait(barrier, nreq - 1 + 3)
@@ -130,7 +133,7 @@
     ssq = jnp.sum(x1 * x1, axis=1, keepdims=True)
     high = ssq.astype(BF).astype(F32)
     low = ssq - high
-    extra = jnp.where(lane == 0, high, jnp.where(lane == 1, low, hot_ref[...]))
+    extra = jnp.where(lane == SSQ0, high, jnp.where(lane == SSQ0 + 1, low, hot_ref[...]))
     yall[tp, blk(me), :CH] = (x1 * gs[tp][:1]).astype(BF)
     yall[tp, blk(me), CH:] = extra.astype(BF)
 
@@ -169,15 +172,18 @@
     total = nreq * rows
     lanes = lax.broadcasted_iota(jnp.int32, (total, EX), 1)
     ssq = jnp.zeros((total, 1), F32)
-    logits = jnp.zeros((total, EX), F32)
+    logits = jnp.zeros((total, EXPERTS), F32)
     for c, (a, w) in enumerate(spans):
         ssq = ssq + jnp.sum(
-            jnp.where(lanes < 2, yall[c, :, CH:].astype(F32), 0.0), axis=1, keepdims=True
-        )
-        logits = logits + jnp.dot(yall[c, :, :w], wr_ref[a:a + w, :], preferred_element_type=F32)
+            jnp.where((lanes >= SSQ0) & (lanes < SSQ0 + 2), yall[c, :, CH:].astype(F32), 0.0), axis=1, keepdims=True
+        )
+        logits = logits + lax.dot_general(
+            yall[c, :, :w], wr_ref[:, a:a + w], NT, preferred_element_type=F32
+        )
     scale = lax.rsqrt(ssq / width + EPS)
     logits = logits * scale
-    hot = (lanes >= HOT0) & (yall[0, :, CH:].astype(F32) > 0.5)
+    experts = lax.broadcasted_iota(jnp.int32, (total, EXPERTS), 1)
+    hot = yall[0, :, CH:CH + EXPERTS].astype(F32) > 0.5
     masked = jnp.where(hot, logits, NEG)
     raw = jnp.where(hot, jnp.exp(masked - jnp.max(masked, axis=1, keepdims=True)), 0.0)
     gates = raw / jnp.sum(raw, axis=1, keepdims=True)
@@ -185,7 +191,7 @@
     hidden = []
     for s in range(slabs):
         weight = jnp.sum(
-            jnp.where(lanes == HOT0 + me * slabs + s, gates, 0.0), axis=1, keepdims=True
+            jnp.where(experts == me * slabs + s, gates, 0.0), axis=1, keepdims=True
         )
         loads[1 + 2 * s].wait()
         loads[2 + 2 * s].wait()
@@ -193,8 +199,8 @@
         up = 0.0
         for c, (a, w) in enumerate(spans):
             y = yall[c, :, :w]
-            gate = gate + jnp.dot(y, wg[s, a:a + w, :], preferred_element_type=F32)
-            up = up + jnp.dot(y, wu[s, a:a + w, :], preferred_element_type=F32)
+            gate = gate + lax.dot_general(y, wg[s, :, a:a + w], NT, preferred_element_type=F32)
+            up = up + lax.dot_general(y, wu[s, :, a:a + w], NT, preferred_element_type=F32)
         gate = jnp.minimum(gate * scale, 7.0)
         up = jnp.clip(up * scale, -7.0, 7.0)
         sig = 1.0 / (1.0 + jnp.exp(-1.702 * gate))
@@ -272,7 +278,7 @@
 
 def tail(att, lin, hot, wo, mg, wr, wg, wu, wd, ng, wq, wk, nreq):
     rows, width = lin.shape
-    slabs, _, ff = wg.shape
+    slabs, ff, _ = wg.shape
     total = nreq * rows
     chunks = -(-width // CH)
     vm = pl.BlockSpec(memory_space=pltpu.VMEM)
@@ -316,6 +322,54 @@
     )(att, lin, hot, wo, mg, wr, wg, wu, wd, ng, wq, wk)
 
 
+def swap_kernel(n, spread, count, *refs):
+    ins, outs, lands = refs[:count], refs[count:2 * count], refs[2 * count:3 * count]
+    ssem, rsem = refs[3 * count:]
+    me = lax.axis_index("req")
+    tp = lax.axis_index("tp")
+    barrier = pltpu.get_barrier_semaphore()
+    for i in range(1, n):
+        pl.semaphore_signal(
+            barrier, inc=1, device_id=((me + i) % n, tp), device_id_type=pl.DeviceIdType.MESH
+        )
+    pl.semaphore_wait(barrier, n - 1)
+    copies = []
+    for i in range(1, n):
+        to = (me + i) % n
+        for a in range(count):
+            cp = pltpu.make_async_remote_copy(
+                src_ref=ins[a].at[to] if spread else ins[a],
+                dst_ref=lands[a].at[me],
+                send_sem=ssem.at[a, i],
+                recv_sem=rsem.at[a, i],
+                device_id=(to, tp),
+                device_id_type=pl.DeviceIdType.MESH,
+            )
+            cp.start()
+            copies.append(cp)
+    for a in range(count):
+        lands[a][me] = ins[a][me] if spread else ins[a][...]
+    for cp in copies:
+        cp.wait()
+    for a in range(count):
+        outs[a][...] = lands[a][...]
+
+
+def swap(arrays, n, spread, ident):
+    vm = pl.BlockSpec(memory_space=pltpu.VMEM)
+    count = len(arrays)
+    shapes = [a.shape if spread else (n,) + a.shape for a in arrays]
+    return pl.pallas_call(
+        functools.partial(swap_kernel, n, spread, count),
+        out_shape=tuple(jax.ShapeDtypeStruct(h, a.dtype) for h, a in zip(shapes, arrays)),
+        in_specs=[vm] * count,
+        out_specs=(vm,) * count,
+        scratch_shapes=[pltpu.VMEM(h, a.dtype) for h, a in zip(shapes, arrays)]
+        + [pltpu.SemaphoreType.DMA((count, n)), pltpu.SemaphoreType.DMA((count, n))],
+        compiler_params=pltpu.CompilerParams(collective_id=ident, has_side_effects=True),
+    )(*arrays)
+
+
 def local(
     layer_in, query_in, key_in, value_in, prompt_keys, prompt_values, gen_keys, gen_values,
     lengths, parents, routes, sinks, out_weight, mlp_gain, router_weight,
@@ -341,7 +395,11 @@
     pos = lens[None, :] + G + jnp.arange(T, dtype=jnp.int32)[:, None]
     q = rope(query_in.astype(F32).reshape(T, B, K * R, HEAD), pos).astype(BF).reshape(T, B, q_width)
     k = rope(key_in.astype(F32).reshape(T, B, K, HEAD), pos).astype(BF).reshape(T, B, kv_width)
-    q_all = lax.all_gather(q, "req", axis_index_groups=groups)
+    direct = span == 1 and lax.axis_size("tp") == 4
+    if direct:
+        (q_all,) = swap([q.reshape(T * B, q_width)], J, False, 1)
+    else:
+        q_all = lax.all_gather(q, "req", axis_index_groups=groups)
     first, tokens = lineage_tables(pars)
     prompt_ok = (beam * S + jnp.arange(S, dtype=jnp.int32))[None, :] < lens[:, None]
     mask = jnp.concatenate(
@@ -368,8 +426,13 @@
     total = total.transpose(2, 3, 0, 1, 4)
     part = (part / jnp.maximum(total, 1e-30)[..., None]).astype(BF)
     stats = jnp.stack([high, total], axis=1)
-    part = lax.all_to_all(part, "req", 0, 0, axis_index_groups=groups)
-    stats = lax.all_to_all(stats, "req", 0, 0, axis_index_groups=groups)
+    if direct:
+        form, table = part.shape, stats.shape
+        part, stats = swap([part.reshape(J, T * B, q_width), stats.reshape(J, -1, 128)], J, True, 2)
+        part, stats = part.reshape(form), stats.reshape(table)
+    else:
+        part = lax.all_to_all(part, "req", 0, 0, axis_index_groups=groups)
+        stats = lax.all_to_all(stats, "req", 0, 0, axis_index_groups=groups)
     high, total = stats[:, 0], stats[:, 1]
     sink = sinks.reshape(K, R)
     peak = jnp.maximum(jnp.max(high, axis=0), sink)
@@ -377,14 +440,13 @@
     bottom = jnp.sum(share, axis=0) + jnp.exp(sink - peak)
     attended = jnp.sum(part.astype(F32) * (share / bottom)[..., None], axis=0)
     attended = attended.astype(BF).reshape(T * B, q_width)
-    if lax.axis_size("tp") == 4 and span == 1 and expert_gate.shape[0] * req_count == EXPERTS:
+    if direct and expert_gate.shape[0] * req_count == EXPERTS:
         hot = jnp.sum(
-            (routes.reshape(T * B, -1, 1) == jnp.arange(EX, dtype=jnp.int32) - HOT0).astype(F32), axis=1
-        )
-        routing = jnp.pad(router_weight, ((0, 0), (HOT0, EX - HOT0 - EXPERTS)))
+            (routes.reshape(T * B, -1, 1) == jnp.arange(EX, dtype=jnp.int32)).astype(F32), axis=1
+        )
         out, nq, nk = tail(
-            attended, layer_in.reshape(T * B, -1), hot, out_weight, mlp_gain[None], routing,
-            expert_gate, expert_up, expert_down, next_gain[None], next_q_weight,
+            attended, layer_in.reshape(T * B, -1), hot, out_weight.T, mlp_gain[None],
+            router_weight.T, jnp.swapaxes(expert_gate, 1, 2), jnp.swapaxes(expert_up, 1, 2), expert_down, next_gain[None], next_q_weight,
             next_kv_weight.reshape(-1, 2 * kv_width), req_count,
         )
         return (

time: 177 us -> 122 us (0.69)
  blocking collectives: 32.5 us -> 0 us
  local copies, waits for them, and re-layouts: 52.3 us -> 21.9 us
  Pallas kernels: 54.7 us -> 80.6 us
  starting transfers between devices: 11.5 us -> 0 us
  waiting for transfers between devices: 5.88 us -> 0 us
    unnamed x34 -> x24, local copies, waits for them, and re-layouts: 38.3 us -> 5.71 us
    all_gather x1 -> x0, blocking collectives: 32.5 us -> none  [local(): q_all = lax.all_gather(q, 'req', axis_index_groups=groups)]
    pallas_call x0 -> x2, Pallas kernels: none -> 24.5 us  [swap(): pl.pallas_call(functools.partial(swap_kernel, n, spread, count), out_shap...]
    all_to_all x2 -> x0, starting transfers between devices: 11.5 us -> none  [the longest x1 6 us: local(): part = lax.all_to_all(part, 'req', 0, 0, axis_index_groups=groups)]
    all_to_all x2 -> x0, waiting for transfers between devices: 5.88 us -> none  [the longest x1 5.88 us: local(): part = lax.all_to_all(part, 'req', 0, 0, axis_index_groups=groups)]
    reshape x0 -> x2, local copies, waits for them, and re-layouts: none -> 2.67 us  [the longest x1 1.66 us: local(): stats.reshape(J, -1, 128)]
  transfers between devices with their start and end apart: 2 -> 0, of which waited for: 1 -> 0; matrix products, arithmetic and copies ran while one was open for 26% -> 0% of each run, Pallas kernels for 0% -> 0%
where the time goes in v2:
time: 122 us; the launch traced here: 119 us
  Pallas kernels  80.6 us (66%)
  local copies, waits for them, and re-layouts  21.9 us (18%)
  other arithmetic  11.1 us (9%)
  matrix products  4.76 us (4%)
    pallas_call x1, Pallas kernels, tail(): pl.pallas_call(functools.partial(tail_kernel, nreq, slabs, width), out_sh...  56.1 us
    pallas_call x2, Pallas kernels, swap(): pl.pallas_call(functools.partial(swap_kernel, n, spread, count), out_shap...  24.5 us
    unnamed x24, local copies, waits for them, and re-layouts  5.71 us
    dot_general x1, matrix products, local(): jnp.einsum('bkjtrs,bskd->jtbkrd', weights.astype(BF), values, preferred_e...  2.59 us

profile of v2, /device:TPU:0, one launch (start us, length us, event | category | flops | bytes accessed | tf_op | source)
XLA Modules:
  0.0 119.4 jit_solution(13428153509505093053)
XLA Ops:
  0.6 0.7 slice_bitcast_fusion.4
  3.0 0.7 select_reduce_fusion.9
  3.8 0.7 broadcast_compare_fusion
  4.7 0.7 broadcast_add_fusion
  5.5 0.8 reshape.182
  6.6 1.2 pad_maximum_fusion.1
  7.8 1.2 copy.86
  9.3 0.7 convert_element_type.38.refs_0_
  10.0 12.2 %shard_map.220 = bf16[8,32,512]{2,1,0:T(8,128)(2,1)} custom-call(bf16[32,512]{1,0:T(8,128)(2,1)} %convert_element_type.38.refs_0_), custom_call_target="tpu_custom_call" | custom-call | tf_op jit(solution)/shard_map/pallas_call | solution.py:362
  22.2 2.1 %reshape.167 = bf16[8,4,8,2,4,64]{5,4,3,2,1,0:T(4,128)(2,1)} reshape(bf16[8,32,512]{2,1,0:T(8,128)(2,1)} %shard_map.220) | data formatting | bytes 524288 | tf_op jit(solution)/shard_map/reshape | solution.py:417
  24.3 2.2 %fusion = (f32[8,2,8,4,4]{2,4,3,1,0:T(4,128)S(1)}, f32[8,2,8,4,4,324]{5,2,4,3,1,0:T(8,128)S(1)}) fusion(pred[8,8,4,324]{3,1,2,0:T(8,128)(4,1)S(1)} %pad_add_fusion, bf16[8,324,2,64,1,1]{1,3,5,4,2,0:T(8,128)(2,1)} %bitcast.109, bf16[8,4,8,2,4,64]{5,4,3,2,1,0:T(4,128)(2,1)} %reshape.167), kind=kOutput, calls=%fused_computation.2 | convolution fusion | flops 86923264 | bytes 3671040 | tf_op jit(solution)/shard_map/jtbkrd,bskd->bkjtrs/dot_general | solution.py:418
  26.5 1.2 %fusion.1 = f32[8,2,8,4,4]{2,4,3,1,0:T(4,128)S(1)} fusion(f32[8,2,8,4,4,324]{5,2,4,3,1,0:T(8,128)S(1)} %get-tuple-element.50, f32[8,2,8,4,4]{2,4,3,1,0:T(4,128)S(1)} %get-tuple-element.49, pred[8,8,4,324]{3,1,2,0:T(8,128)(4,1)S(1)} %pad_add_fusion), kind=kLoop, calls=%fused_computation.3 | loop fusion | flops 3315712 | bytes 2753536 | tf_op jit(solution)/shard_map/reduce_sum | solution.py:423
  27.8 0.7 copy.89
  28.5 1.7 %copy.90.refs_1_ = f32[8,4,128]{2,1,0:T(4,128)} copy(f32[8,4,128]{0,2,1:T(8,128)} %bitcast.114) | data formatting | bytes 32768 | tf_op jit(solution)/shard_map/reshape | solution.py:431
  30.2 0.7 bitcast_maximum_fusion
  30.9 2.0 %pad_maximum_fusion = bf16[8,324,128]{2,1,0:T(8,128)(2,1)} fusion(bf16[8,4,128]{2,1,0:T(4,128)(2,1)S(1)} %bitcast.132, bf16[8,64,128]{2,1,0:T(8,128)(2,1)} %param.28, bf16[8,256,128]{2,1,0:T(8,128)(2,1)} %param.26), kind=kLoop, calls=%fused_computation.14 | loop fusion | flops 1990656 | bytes 1327104 | tf_op jit(solution)/shard_map/concatenate | solution.py:414
  32.9 2.2 %copy.79 = bf16[8,324,128]{1,2,0:T(8,128)(2,1)} copy(bf16[8,324,128]{2,1,0:T(8,128)(2,1)} %pad_maximum_fusion) | data formatting | bytes 1327104 | tf_op jit(solution)/shard_map/concatenate | solution.py:414
  35.1 2.6 %divide_convert_fusion = bf16[8,4,8,2,4,64]{5,0,4,1,3,2:T(8,128)(2,1)S(1)} fusion(bf16[8,324,2,64,1,1]{1,3,5,4,2,0:T(8,128)(2,1)} %bitcast.115, f32[8,2,8,4,4,324]{5,2,4,3,1,0:T(8,128)S(1)} %get-tuple-element.50, f32[8,2,8,4,4]{2,4,3,1,0:T(4,128)S(1)} %get-tuple-element.49, pred[8,8,4,324]{3,1,2,0:T(8,128)(4,1)S(1)} %pad_add_fusion, ...), kind=kOutput, calls=%fused_computation.13 | convolution fusion | flops 88514560 | bytes 3679232 | tf_op jit(solution)/shard_map/bkjtrs,bskd->jtbkrd/dot_general | solution.py:424
  38.0 1.0 reshape.171.refs_0_
  39.0 12.3 %shard_map.221 = (bf16[8,32,512]{2,1,0:T(8,128)(2,1)}, f32[8,4,128]{2,1,0:T(4,128)}) custom-call(bf16[8,32,512]{2,1,0:T(8,128)(2,1)} %reshape.171.refs_0_, f32[8,4,128]{2,1,0:T(4,128)} %copy.90.refs_1_), custom_call_target="tpu_custom_call" | custom-call | tf_op jit(solution)/shard_map/pallas_call | solution.py:362
  51.3 0.9 copy.91
  53.7 0.6 mul.140
  54.3 0.7 mul.141
  55.0 0.7 multiply_reduce_fusion.att_ref
  55.7 1.3 %copy.110 = bf16[360,8,2,128]{3,1,2,0:T(8,128)(2,1)} copy(bf16[360,8,2,128]{3,2,1,0:T(2,128)(2,1)S(1)} %bitcast.111) | data formatting | bytes 2949120
  57.1 0.7 convert_reduce_fusion.hot_ref
  57.8 0.6 broadcast_in_dim.143.mg_ref
  58.4 0.6 broadcast_in_dim.144.ng_ref
  59.0 56.1 %shard_map.222 = (bf16[32,2880]{1,0:T(8,128)(2,1)}, bf16[32,512]{1,0:T(8,128)(2,1)}, bf16[32,256]{1,0:T(8,128)(2,1)}) custom-call(bf16[32,512]{1,0:T(8,128)(2,1)} %multiply_reduce_fusion.att_ref, bf16[32,2880]{1,0:T(8,128)(2,1)} %bitcast.120, f32[32,128]{1,0:T(8,128)} %convert_reduce_fusion.hot_ref, bf16[2880,512]{1,0:T(8,128)(2,1)} %bitcast.110, ...), custom_call_target="tpu_custom_call" | custom-call | flops 6370099200 | bytes 34603008 | tf_op jit(solution)/shard_map/pallas_call | solution.py:287
  115.1 1.3 %copy.94 = bf16[4,8,2,128]{3,2,1,0:T(2,128)(2,1)} copy(bf16[4,8,2,128]{3,1,2,0:T(8,128)(2,1)} %bitcast.136) | data formatting | bytes 32768
  116.4 1.6 %copy.114 = bf16[4,8,2880]{2,1,0:T(8,128)(2,1)} copy(bf16[4,8,2880]{2,1,0:T(8,128)(2,1)} %bitcast.121) | data formatting | bytes 368640
  118.1 1.4 %copy.115 = bf16[4,8,512]{2,1,0:T(8,128)(2,1)} copy(bf16[4,8,512]{2,1,0:T(8,128)(2,1)} %bitcast.133) | data formatting | bytes 65536
  (60 shorter events, 4.4 us)
Async XLA Ops:
  0.6 8.3 %copy-start.2 = (bf16[4,8,512]{2,1,0:T(8,128)(2,1)S(1)}, bf16[4,8,512]{2,1,0:T(8,128)(2,1)}, u32[]{:S(2)}) copy-start(bf16[4,8,512]{2,1,0:T(8,128)(2,1)} %param.22) | copy-start | bytes 98308
  26.4 4.4 %copy-start.5 = (bf16[4,8,128]{2,1,0:T(8,128)(2,1)S(1)}, bf16[4,8,128]{2,1,0:T(8,128)(2,1)}, u32[]{:S(2)}) copy-start(bf16[4,8,128]{2,1,0:T(8,128)(2,1)} %param.24) | copy-start | bytes 24580
  35.1 17.3 %copy-start.7 = (f32[8]{0:T(128)S(1)}, f32[8]{0:T(128)}, u32[]{:S(2)}) copy-start(f32[8]{0:T(128)} %param.32) | copy-start | bytes 100
  38.0 17.6 %copy-start = (bf16[2880,2,128]{2,1,0:T(2,128)(2,1)S(1)}, bf16[2880,2,128]{2,1,0:T(2,128)(2,1)}, u32[]{:S(2)}) copy-start(bf16[2880,2,128]{2,1,0:T(2,128)(2,1)} %param.41) | copy-start | bytes 4423684
  51.3 3.6 %copy-start.1 = (bf16[8,32,512]{2,1,0:T(8,128)(2,1)S(1)}, bf16[8,32,512]{2,1,0:T(8,128)(2,1)}, u32[]{:S(2)}) copy-start(bf16[8,32,512]{2,1,0:T(8,128)(2,1)} %get-tuple-element.8) | copy-start | bytes 786436
  53.6 3.3 %copy-start.6 = (s32[4,8,4]{1,2,0:T(4,128)S(1)}, s32[4,8,4]{1,2,0:T(4,128)}, u32[]{:S(2)}) copy-start(s32[4,8,4]{1,2,0:T(4,128)} %param.31) | copy-start | bytes 1540
  53.7 4.1 %copy-start.3 = (f32[2880]{0:T(1024)S(1)}, f32[2880]{0:T(1024)}, u32[]{:S(2)}) copy-start(f32[2880]{0:T(1024)} %param.34) | copy-start | bytes 34564
  53.7 4.7 %copy-start.4 = (f32[2880]{0:T(1024)S(1)}, f32[2880]{0:T(1024)}, u32[]{:S(2)}) copy-start(f32[2880]{0:T(1024)} %param.39) | copy-start | bytes 34564
